TPU v7x, 32 devices: a whole 2x2x4 slice. The times are simulated.
32 devices in a mesh: head: 4 (over z), page: 8 (over y, x, core).
Axes of the slice: x: 2, y: 2, z: 4, core: 2. Of those that a mesh axis runs over, the one named last changes fastest.
Arguments:
- hidden_in: bfloat16 [8, 1024, 1024], P('page', 'head'), may hold values from -6 to 6
- norm_gain: float32 [1024], replicated, may hold values from 0.1 to 1.9
- w_qkv: bfloat16 [1024, 3, 1024], P(None, None, 'head'), may hold values from -0.1875 to 0.1875
- w_out: bfloat16 [1024, 1024], P('head'), may hold values from -0.75 to 0.75
- cache_kv: bfloat16 [2, 16, 128, 1024], P(None, 'page', None, 'head'), may hold values from -110 to 110, as said below
- page_node: int32 [16], replicated, may hold values from 0 to 6, as said below
- page_fill: int32 [16], replicated, may hold values from 1 to 128
- node_parent: int32 [7], replicated, may hold values from 0 to 2, as said below
- tok_seg: int32 [8, 1024], P('page'), may hold values from 0 to 7, never falling along the last dimension, each value on 1 to 256 neighbouring positions
- req_leaf: int32 [8, 8], P('page'), may hold values from 3 to 6, as said below
Outputs:
- attn_out: bfloat16 [8, 1024, 1024], P('page', 'head')
Inputs may be any that keep to these rules, and one draw needn't show every extreme that they name: `cache_kv`: entries of the cache; keys and values. `page_node`: every node owns at least one page. `node_parent`: node 0 is the root and its own parent; nodes 1 to 2 have parent 0; the others have a parent among nodes 1 to 2, and each of those has a child. `req_leaf`: each request names a lowest-level node; every lowest-level node is named by some request.
All inputs are finite; a program needn't handle non-finite values.
Results may differ from a plain program's by a relative error of at most 0.018.
Values may be sent and summed in bfloat16 or wider, within the bound.
A program may use at most 64 MiB of HBM per device.

v0:
```python
import math

import jax
import jax.numpy as jnp
from jax import lax
from jax.sharding import PartitionSpec as P

HD = 64


EPSILON = 1e-06
FLOOR_SCORE = -1e30


def lookup(indices, lookup_table):
    matches = indices[:, None] == jnp.arange(lookup_table.shape[0], dtype=jnp.int32)[None, :]
    return jnp.sum(jnp.where(matches, lookup_table[None, :], 0), axis=1)


def shards(
    hidden_in,
    norm_gain,
    w_qkv,
    w_out,
    cache_kv,
    page_node,
    page_fill,
    node_parent,
    tok_seg,
    req_leaf,
):
    widened = hidden_in[0].astype(jnp.float32)
    normed = (
        widened
        * lax.rsqrt(jnp.mean(widened * widened, axis=1, keepdims=True) + EPSILON)
        * norm_gain
    ).astype(jnp.bfloat16)
    model_width = widened.shape[1]
    group_width = w_qkv.shape[2]
    head_size = HD
    group_heads = group_width // head_size
    weight_flat = w_qkv.reshape(model_width, 3 * group_width)
    projected = jnp.dot(
        lax.all_gather(normed, "head", axis=0, tiled=True),
        weight_flat,
        preferred_element_type=jnp.float32,
    ).astype(jnp.bfloat16)
    queries_all = projected.shape[0]
    queries = projected[:, :group_width].reshape(queries_all, group_heads, head_size)
    key_new = projected[:, group_width : 2 * group_width].reshape(
        queries_all, group_heads, head_size
    )
    value_new = projected[:, 2 * group_width :].reshape(queries_all, group_heads, head_size)
    score_scale = head_size ** (-0.5)
    segment = tok_seg[0]
    leaf_node = lookup(segment, req_leaf[0])
    upper_node = lookup(leaf_node, node_parent)
    root_node = lookup(upper_node, node_parent)
    position = jnp.arange(queries_all, dtype=jnp.int32)
    block_rows = min(queries_all, 512)

    def suffix_block(first):
        query_rows = lax.dynamic_slice_in_dim(queries, first, block_rows, 0)
        segment_rows = lax.dynamic_slice_in_dim(segment, first, block_rows, 0)
        position_rows = first + jnp.arange(block_rows, dtype=jnp.int32)
        visible = (segment_rows[:, None] == segment[None, :]) & (
            position[None, :] <= position_rows[:, None]
        )
        scores = (
            jnp.einsum("qhd,khd->hqk", query_rows, key_new, preferred_element_type=jnp.float32)
            * score_scale
        )
        scores = jnp.where(visible[None], scores, FLOOR_SCORE)
        row_max = jnp.max(scores, axis=2)
        weights = jnp.where(visible[None], jnp.exp(scores - row_max[:, :, None]), 0.0)
        row_sum = jnp.sum(weights, axis=2)
        weighted = jnp.einsum(
            "hqk,khd->hqd",
            weights.astype(jnp.bfloat16),
            value_new,
            preferred_element_type=jnp.float32,
        )
        return (row_max, row_sum, weighted)

    block_starts = jnp.arange(0, queries_all, block_rows, dtype=jnp.int32)
    block_max, block_sum, block_weighted = lax.map(suffix_block, block_starts)
    initial = (
        jnp.transpose(block_max, (1, 0, 2)).reshape(group_heads, queries_all),
        jnp.transpose(block_sum, (1, 0, 2)).reshape(group_heads, queries_all),
        jnp.transpose(block_weighted, (1, 0, 2, 3)).reshape(group_heads, queries_all, head_size),
    )
    page_len = cache_kv.shape[2]
    page_slot = jnp.arange(page_len, dtype=jnp.int32)
    shard_piece = lax.all_gather(cache_kv, "page", axis=1, tiled=True)
    piece_pages = shard_piece.shape[1]
    group_pages = math.gcd(piece_pages, 4)
    step_count = piece_pages // group_pages
    block_keys = group_pages * page_len
    key_blocks = shard_piece[0].reshape(step_count, block_keys, group_heads, head_size)
    value_blocks = shard_piece[1].reshape(step_count, block_keys, group_heads, head_size)
    key_nodes = jnp.repeat(page_node, page_len).reshape(step_count, block_keys)
    key_valid = (page_slot[None, :] < page_fill[:, None]).reshape(step_count, block_keys)

    def one_step(partial_value, inputs):
        row_max, row_sum, weighted = partial_value
        key_block, value_block, node_block, valid_block = inputs
        visible = (
            (node_block[None, :] == leaf_node[:, None])
            | (node_block[None, :] == upper_node[:, None])
            | (node_block[None, :] == root_node[:, None])
        ) & valid_block[None, :]
        scores = (
            jnp.einsum("qhd,khd->hqk", queries, key_block, preferred_element_type=jnp.float32)
            * score_scale
        )
        scores = jnp.where(visible[None], scores, FLOOR_SCORE)
        new_max = jnp.maximum(row_max, jnp.max(scores, axis=2))
        rescale = jnp.exp(row_max - new_max)
        weights = jnp.where(visible[None], jnp.exp(scores - new_max[:, :, None]), 0.0)
        row_sum = row_sum * rescale + jnp.sum(weights, axis=2)
        weighted = weighted * rescale[:, :, None] + jnp.einsum(
            "hqk,khd->hqd",
            weights.astype(jnp.bfloat16),
            value_block,
            preferred_element_type=jnp.float32,
        )
        return ((new_max, row_sum, weighted), None)

    result_state, unused = lax.scan(
        one_step, initial, (key_blocks, value_blocks, key_nodes, key_valid)
    )
    final_max, final_sum, final_weighted = result_state
    attention = (final_weighted / final_sum[:, :, None]).astype(jnp.bfloat16)
    attention = jnp.transpose(attention, (1, 0, 2)).reshape(queries_all, group_width)
    result = lax.psum_scatter(
        jnp.dot(attention, w_out, preferred_element_type=jnp.float32).astype(jnp.bfloat16),
        "head",
        scatter_dimension=0,
        tiled=True,
    )
    return result[None]


def solution(mesh):
    placed = (
        P("page", "head", None),
        P(),
        P(None, None, "head"),
        P("head", None),
        P(None, "page", None, "head"),
        P(),
        P(),
        P(),
        P("page", None),
        P("page", None),
    )
    return jax.shard_map(
        shards, mesh=mesh, in_specs=placed, out_specs=P("page", "head", None), check_vma=False
    )
```

profile of v0, /device:TPU:0, one launch (start us, length us, event | category | flops | bytes accessed | tf_op | source)
XLA Modules:
  0.0 196.2 jit_solution(5390336765327780375)
XLA Ops:
  16.4 42.3 %all-gather.3.cloned.1.call-done = bf16[1024,1024]{1,0:T(8,128)(2,1)} async-done(((bf16[256,1024]{1,0:T(8,128)(2,1)}), bf16[1024,1024]{1,0:T(8,128)(2,1)}) %all-gather.3.cloned.1.call-update) | async-done | bytes 2097168 | tf_op jit(solution)/shard_map/all_gather | solution.py:44
  58.7 3.4 %convolution_convert_fusion.1 = bf16[1024,768]{0,1:T(8,128)(2,1)S(1)} fusion(bf16[1024,1024]{1,0:T(8,128)(2,1)} %all-gather.3.cloned.1.call-done, bf16[1024,768]{0,1:T(8,128)(2,1)S(1)} %bitcast.108), kind=kOutput, calls=%fused_computation.45 | convolution fusion | flops 1611399168 | bytes 5242880 | tf_op jit(solution)/shard_map/dot_general | solution.py:43
  63.0 24.4 %while.30 = (s32[]{:T(128)}, f32[2,4,512]{2,1,0:T(4,128)S(1)}, f32[2,4,512]{2,1,0:T(4,128)S(1)}, f32[2,4,512,64]{2,3,1,0:T(8,128)S(1)}, s32[2]{0:T(128)S(1)}, /*...) while((s32[]{:T(128)}, f32[2,4,512]{2,1,0:T(4,128)S(1)}, ...), condition=%wide.region_4.5_spmd.clone, body=%wide.region_1.4_spmd.clone.sunk | while | flops 565703168 | bytes 29178048 | solution.py:86
  68.7 3.6 %fusion.77 = f32[2,4,512,64]{2,3,1,0:T(8,128)S(1)} fusion(f32[2,4,512,64]{2,3,1,0:T(8,128)S(1)} %get-tuple-element.401, s32[]{:T(128)} %get-tuple-element.398, bf16[1024,4,64]{0,2,1:T(8,128)(2,1)} %get-tuple-element.420, f32[4,512,1024]{2,1,0:T(8,128)S(1)} %get-tuple-element.381, f32[4,512]{1,0:T(4,128)S(1)} %get-tuple-element.382, ...), kind=kOutput, calls=%fused_computation.11.clone.1 | convolution fusion | flops 278921216 | bytes 9969668 | tf_op jit(solution)/shard_map/while/body/eval_jaxpr/hqk,khd->hqd/dot_general | solution.py:77
  72.3 2.9 %fusion.76 = f32[4,512]{1,0:T(4,128)S(1)} fusion(f32[4,512,1024]{2,1,0:T(8,128)S(1)} %get-tuple-element.381, f32[4,512]{1,0:T(4,128)S(1)} %get-tuple-element.382, pred[512,1024]{1,0:T(8,128)(4,1)S(1)} %fusion.74), kind=kLoop, calls=%fused_computation.5.clone.1 | loop fusion | flops 10483712 | bytes 8929280 | tf_op jit(solution)/shard_map/while/body/eval_jaxpr/reduce_sum | solution.py:76
  80.9 3.6 %fusion.77 = f32[2,4,512,64]{2,3,1,0:T(8,128)S(1)} fusion(f32[2,4,512,64]{2,3,1,0:T(8,128)S(1)} %get-tuple-element.401, s32[]{:T(128)} %get-tuple-element.398, bf16[1024,4,64]{0,2,1:T(8,128)(2,1)} %get-tuple-element.420, f32[4,512,1024]{2,1,0:T(8,128)S(1)} %get-tuple-element.381, f32[4,512]{1,0:T(4,128)S(1)} %get-tuple-element.382, ...), kind=kOutput, calls=%fused_computation.11.clone.1 | convolution fusion | flops 278921216 | bytes 9969668 | tf_op jit(solution)/shard_map/while/body/eval_jaxpr/hqk,khd->hqd/dot_general | solution.py:77
  84.5 2.9 %fusion.76 = f32[4,512]{1,0:T(4,128)S(1)} fusion(f32[4,512,1024]{2,1,0:T(8,128)S(1)} %get-tuple-element.381, f32[4,512]{1,0:T(4,128)S(1)} %get-tuple-element.382, pred[512,1024]{1,0:T(8,128)(4,1)S(1)} %fusion.74), kind=kLoop, calls=%fused_computation.5.clone.1 | loop fusion | flops 10483712 | bytes 8929280 | tf_op jit(solution)/shard_map/while/body/eval_jaxpr/reduce_sum | solution.py:76
  88.5 3.1 %fusion.43 = (bf16[1,16,128,256]{3,2,1,0:T(8,128)(2,1)}, bf16[1,16,128,256]{3,2,1,0:T(8,128)(2,1)}) fusion(bf16[2,16,128,256]{3,2,1,0:T(8,128)(2,1)} %all-gather.5.cloned.1.call-done), kind=kLoop, calls=%fused_computation.65 | loop fusion | bytes 4194304 | tf_op jit(solution)/shard_map/slice | solution.py:100
  91.6 3.3 %reshape.224 = bf16[4,512,4,64]{3,2,1,0:T(4,128)(2,1)S(1)} reshape(bf16[1,16,128,256]{3,2,1,0:T(8,128)(2,1)} %get-tuple-element.231) | data formatting | bytes 2097152 | tf_op jit(solution)/shard_map/reshape;squeeze | solution.py:99
  94.9 2.3 %copy.24 = bf16[4,512,4,64]{1,3,2,0:T(8,128)(2,1)} copy(bf16[4,512,4,64]{3,2,1,0:T(4,128)(2,1)S(1)} %reshape.224) | data formatting | bytes 2097152 | tf_op jit(solution)/shard_map/while | solution.py:129
  97.3 3.3 %reshape.225 = bf16[4,512,4,64]{3,2,1,0:T(4,128)(2,1)S(1)} reshape(bf16[1,16,128,256]{3,2,1,0:T(8,128)(2,1)} %get-tuple-element.230) | data formatting | bytes 2097152 | tf_op jit(solution)/shard_map/reshape;squeeze | solution.py:100
  100.6 2.4 %copy.25 = bf16[4,512,4,64]{1,3,2,0:T(8,128)(2,1)} copy(bf16[4,512,4,64]{3,2,1,0:T(4,128)(2,1)S(1)} %reshape.225) | data formatting | bytes 2097152 | tf_op jit(solution)/shard_map/while | solution.py:129
  102.9 40.5 %while.29 = (s32[]{:T(128)}, f32[4,1024]{1,0:T(4,128)S(1)}, f32[4,1024]{1,0:T(4,128)S(1)}, f32[4,1024,64]{1,2,0:T(8,128)}, s32[4,512]{1,0:T(4,128)S(1)}, /*index...) while((s32[]{:T(128)}, f32[4,1024]{1,0:T(4,128)S(1)}, ...), condition=%wide.region_11.12_spmd, body=%wide.region_8.11_spmd.sunk | while | flops 567812096 | bytes 39080636 | solution.py:129
  103.6 2.6 %fusion.68 = (f32[4,1024]{1,0:T(4,128)S(1)}, f32[4,512,1024]{2,1,0:T(8,128)S(1)}) fusion(pred[1024,512]{0,1:T(8,128)(4,1)S(1)} %or_and_fusion.2, bf16[1024,4,64]{0,2,1:T(8,128)(2,1)S(1)} %get-tuple-element.460, bf16[4,512,4,64]{1,3,2,0:T(8,128)(2,1)} %get-tuple-element.459, s32[]{:T(128)} %get-tuple-element.437), kind=kOutput, calls=%fused_computation.23.clone.1 | convolution fusion | flops 274722816 | bytes 9716224 | tf_op jit(solution)/shard_map/while/body/eval_jaxpr/qhd,khd->hqk/dot_general | solution.py:113
  106.3 2.1 %fusion.69 = f32[4,1024]{1,0:T(4,128)S(1)} fusion(f32[4,512,1024]{2,1,0:T(8,128)S(1)} %get-tuple-element.368, f32[4,1024]{1,0:T(4,128)S(1)} %max.4, pred[1024,512]{0,1:T(8,128)(4,1)S(1)} %or_and_fusion.2), kind=kLoop, calls=%fused_computation.25.clone.1 | loop fusion | flops 10481664 | bytes 8945664 | tf_op jit(solution)/shard_map/while/body/eval_jaxpr/reduce_sum | solution.py:120
  108.4 3.6 %fusion.70 = f32[4,1024,64]{1,2,0:T(8,128)S(1)} fusion(f32[4,512,1024]{2,1,0:T(8,128)S(1)} %get-tuple-element.368, f32[4,1024]{1,0:T(4,128)S(1)} %max.4, pred[1024,512]{0,1:T(8,128)(4,1)S(1)} %or_and_fusion.2, f32[4,1024,64]{1,2,0:T(8,128)S(1)} %copy-done.1, f32[4,1024]{1,0:T(4,128)S(1)} %get-tuple-element.370, ...), kind=kOutput, calls=%fused_computation.29.clone.1 | convolution fusion | flops 279445504 | bytes 11305472 | tf_op jit(solution)/shard_map/while/body/eval_jaxpr/hqk,khd->hqd/dot_general | solution.py:121
  113.7 2.6 %fusion.68 = (f32[4,1024]{1,0:T(4,128)S(1)}, f32[4,512,1024]{2,1,0:T(8,128)S(1)}) fusion(pred[1024,512]{0,1:T(8,128)(4,1)S(1)} %or_and_fusion.2, bf16[1024,4,64]{0,2,1:T(8,128)(2,1)S(1)} %get-tuple-element.460, bf16[4,512,4,64]{1,3,2,0:T(8,128)(2,1)} %get-tuple-element.459, s32[]{:T(128)} %get-tuple-element.437), kind=kOutput, calls=%fused_computation.23.clone.1 | convolution fusion | flops 274722816 | bytes 9716224 | tf_op jit(solution)/shard_map/while/body/eval_jaxpr/qhd,khd->hqk/dot_general | solution.py:113
  116.4 2.1 %fusion.69 = f32[4,1024]{1,0:T(4,128)S(1)} fusion(f32[4,512,1024]{2,1,0:T(8,128)S(1)} %get-tuple-element.368, f32[4,1024]{1,0:T(4,128)S(1)} %max.4, pred[1024,512]{0,1:T(8,128)(4,1)S(1)} %or_and_fusion.2), kind=kLoop, calls=%fused_computation.25.clone.1 | loop fusion | flops 10481664 | bytes 8945664 | tf_op jit(solution)/shard_map/while/body/eval_jaxpr/reduce_sum | solution.py:120
  118.5 3.6 %fusion.70 = f32[4,1024,64]{1,2,0:T(8,128)S(1)} fusion(f32[4,512,1024]{2,1,0:T(8,128)S(1)} %get-tuple-element.368, f32[4,1024]{1,0:T(4,128)S(1)} %max.4, pred[1024,512]{0,1:T(8,128)(4,1)S(1)} %or_and_fusion.2, f32[4,1024,64]{1,2,0:T(8,128)S(1)} %copy-done.1, f32[4,1024]{1,0:T(4,128)S(1)} %get-tuple-element.370, ...), kind=kOutput, calls=%fused_computation.29.clone.1 | convolution fusion | flops 279445504 | bytes 11305472 | tf_op jit(solution)/shard_map/while/body/eval_jaxpr/hqk,khd->hqd/dot_general | solution.py:121
  123.8 2.6 %fusion.68 = (f32[4,1024]{1,0:T(4,128)S(1)}, f32[4,512,1024]{2,1,0:T(8,128)S(1)}) fusion(pred[1024,512]{0,1:T(8,128)(4,1)S(1)} %or_and_fusion.2, bf16[1024,4,64]{0,2,1:T(8,128)(2,1)S(1)} %get-tuple-element.460, bf16[4,512,4,64]{1,3,2,0:T(8,128)(2,1)} %get-tuple-element.459, s32[]{:T(128)} %get-tuple-element.437), kind=kOutput, calls=%fused_computation.23.clone.1 | convolution fusion | flops 274722816 | bytes 9716224 | tf_op jit(solution)/shard_map/while/body/eval_jaxpr/qhd,khd->hqk/dot_general | solution.py:113
  128.6 3.6 %fusion.70 = f32[4,1024,64]{1,2,0:T(8,128)S(1)} fusion(f32[4,512,1024]{2,1,0:T(8,128)S(1)} %get-tuple-element.368, f32[4,1024]{1,0:T(4,128)S(1)} %max.4, pred[1024,512]{0,1:T(8,128)(4,1)S(1)} %or_and_fusion.2, f32[4,1024,64]{1,2,0:T(8,128)S(1)} %copy-done.1, f32[4,1024]{1,0:T(4,128)S(1)} %get-tuple-element.370, ...), kind=kOutput, calls=%fused_computation.29.clone.1 | convolution fusion | flops 279445504 | bytes 11305472 | tf_op jit(solution)/shard_map/while/body/eval_jaxpr/hqk,khd->hqd/dot_general | solution.py:121
  133.9 2.6 %fusion.68 = (f32[4,1024]{1,0:T(4,128)S(1)}, f32[4,512,1024]{2,1,0:T(8,128)S(1)}) fusion(pred[1024,512]{0,1:T(8,128)(4,1)S(1)} %or_and_fusion.2, bf16[1024,4,64]{0,2,1:T(8,128)(2,1)S(1)} %get-tuple-element.460, bf16[4,512,4,64]{1,3,2,0:T(8,128)(2,1)} %get-tuple-element.459, s32[]{:T(128)} %get-tuple-element.437), kind=kOutput, calls=%fused_computation.23.clone.1 | convolution fusion | flops 274722816 | bytes 9716224 | tf_op jit(solution)/shard_map/while/body/eval_jaxpr/qhd,khd->hqk/dot_general | solution.py:113
  138.8 3.6 %fusion.70 = f32[4,1024,64]{1,2,0:T(8,128)S(1)} fusion(f32[4,512,1024]{2,1,0:T(8,128)S(1)} %get-tuple-element.368, f32[4,1024]{1,0:T(4,128)S(1)} %max.4, pred[1024,512]{0,1:T(8,128)(4,1)S(1)} %or_and_fusion.2, f32[4,1024,64]{1,2,0:T(8,128)S(1)} %copy-done.1, f32[4,1024]{1,0:T(4,128)S(1)} %get-tuple-element.370, ...), kind=kOutput, calls=%fused_computation.29.clone.1 | convolution fusion | flops 279445504 | bytes 11305472 | tf_op jit(solution)/shard_map/while/body/eval_jaxpr/hqk,khd->hqd/dot_general | solution.py:121
  146.9 42.8 %reduce-scatter.2.cloned.1.call-done = bf16[256,1024]{1,0:T(8,128)(2,1)} async-done(((bf16[1024,1024]{1,0:T(8,128)(2,1)}), bf16[256,1024]{1,0:T(8,128)(2,1)}) %reduce-scatter.2.cloned.1.call-update) | async-done | bytes 524304 | tf_op jit(solution)/shard_map/reduce_scatter | solution.py:135
  (87 shorter events, 33.7 us)
Async XLA Ops:
  6.5 138.2 %copy-start = (bf16[256,1024]{1,0:T(8,128)(2,1)S(1)}, bf16[256,1024]{1,0:T(8,128)(2,1)}, u32[]{:S(2)}) copy-start(bf16[256,1024]{1,0:T(8,128)(2,1)} %param.17) | copy-start | bytes 1572868
  6.5 52.1 %all-gather.3.cloned.1.call-start = ((), (), s32[]{:S(2)}) async-start(), calls=%async_computation.1 | async-start | bytes 2621440 | tf_op jit(solution)/shard_map/all_gather | solution.py:44
  9.9 78.6 %all-gather.5.cloned.1.call-start = ((), (), s32[]{:S(2)}) async-start(), calls=%async_computation.2 | async-start | bytes 2359296 | tf_op jit(solution)/shard_map/all_gather | solution.py:94
  10.6 179.0 %reduce-scatter.2.cloned.1.call-start = ((), (), s32[]{:S(2)}) async-start(), calls=%async_computation.3 | async-start | bytes 2621440 | tf_op jit(solution)/shard_map/reduce_scatter | solution.py:135
  10.7 52.3 %copy-start.3 = (s32[1,1024]{1,0:T(1,128)S(1)}, s32[1,1024]{1,0:T(1,128)}, u32[]{:S(2)}) copy-start(s32[1,1024]{1,0:T(1,128)} %param.22) | copy-start | bytes 12292
  103.6 4.8 %copy-start.1 = (f32[4,1024,64]{1,2,0:T(8,128)S(1)}, f32[4,1024,64]{1,2,0:T(8,128)}, u32[]{:S(2)}) copy-start(f32[4,1024,64]{1,2,0:T(8,128)} %get-tuple-element.440) | copy-start | bytes 3145732 | tf_op jit(solution)/shard_map/while
  112.1 1.0 copy-start.2
  113.7 4.8 %copy-start.1 = (f32[4,1024,64]{1,2,0:T(8,128)S(1)}, f32[4,1024,64]{1,2,0:T(8,128)}, u32[]{:S(2)}) copy-start(f32[4,1024,64]{1,2,0:T(8,128)} %get-tuple-element.440) | copy-start | bytes 3145732 | tf_op jit(solution)/shard_map/while
  122.2 1.0 copy-start.2
  123.8 4.8 %copy-start.1 = (f32[4,1024,64]{1,2,0:T(8,128)S(1)}, f32[4,1024,64]{1,2,0:T(8,128)}, u32[]{:S(2)}) copy-start(f32[4,1024,64]{1,2,0:T(8,128)} %get-tuple-element.440) | copy-start | bytes 3145732 | tf_op jit(solution)/shard_map/while
  132.3 1.0 copy-start.2
  133.9 4.8 %copy-start.1 = (f32[4,1024,64]{1,2,0:T(8,128)S(1)}, f32[4,1024,64]{1,2,0:T(8,128)}, u32[]{:S(2)}) copy-start(f32[4,1024,64]{1,2,0:T(8,128)} %get-tuple-element.440) | copy-start | bytes 3145732 | tf_op jit(solution)/shard_map/while
  142.4 1.0 copy-start.2
Sparse Core Ops, SparseCore 0:
  10.0 48.6 all-gather.2
  60.6 26.6 all-gather.4
  147.0 42.6 reduce-scatter.1
where the time goes:
time: 197 us; the launch traced here: 196 us
  waiting for transfers between devices  85.8 us (44%)
  matrix products  41.7 us (21%)
  other arithmetic  26.1 us (13%)
  local copies, waits for them, and re-layouts  25.2 us (13%)
  between operations  13.2 us (7%)
  loops' own time  4.01 us (2%)
    reduce_scatter x1, waiting for transfers between devices, shards(): lax.psum_scatter(jnp.dot(attention, w_out, preferred_element_type=jnp.flo...  42.8 us
    all_gather x1, waiting for transfers between devices, shards(): lax.all_gather(normed, 'head', axis=0, tiled=True)  42.3 us
    dot_general x4, matrix products, one_step(): jnp.einsum('hqk,khd->hqd', weights.astype(jnp.bfloat16), value_block, pre...  14.6 us
    dot_general x4, matrix products, one_step(): jnp.einsum('qhd,khd->hqk', queries, key_block, preferred_element_type=jnp...  10.6 us
    reduce_sum x4, other arithmetic, one_step(): row_sum = row_sum * rescale + jnp.sum(weights, axis=2)  8.44 us
    dot_general x2, matrix products, suffix_block(): jnp.einsum('hqk,khd->hqd', weights.astype(jnp.bfloat16), value_new, prefe...  7.1 us
    reduce_sum x2, other arithmetic, suffix_block(): row_sum = jnp.sum(weights, axis=2)  5.82 us
    while x2, local copies, waits for them, and re-layouts, shards(): lax.scan(one_step, initial, (key_blocks, value_blocks, key_nodes, key_val...  4.68 us
  transfers between devices with their start and end apart: 3, of which 2 were waited for; matrix products, arithmetic and copies ran while one was open for 16% of the time, Pallas kernels for 0%

commit v1 on v0

v1 whole, which is shorter than its diff:
```python
import functools

import jax
import jax.numpy as jnp
from jax import lax
from jax.experimental import pallas as pl
from jax.experimental.pallas import tpu as pltpu
from jax.sharding import PartitionSpec as P

HD = 64
EPSILON = 1e-06
BIG = 1e30
KEY_BLOCK = 2048
SPLIT = 8
MESH = pl.DeviceIdType.MESH
F32 = jnp.float32
BF16 = jnp.bfloat16


def dot_t(a, b):
    return lax.dot_general(a, b, (((1,), (1,)), ((), ())), preferred_element_type=F32)


def dot(a, b):
    return jnp.dot(a, b, preferred_element_type=F32)


def kernel(
    dims,
    hid,
    gain,
    w,
    wo,
    cache,
    page_node,
    page_fill,
    parent,
    seg,
    leaf,
    out,
    normed,
    cache_all,
    wo_rel,
    qa,
    ka,
    va,
    kp,
    vp,
    acc,
    top,
    qext,
    kext,
    attn,
    attn_rel,
    x_send,
    x_recv,
    c_send,
    c_fwd,
    c_recv,
    wz_send,
    wz_recv,
    wp_send,
    wp_recv,
    a_send,
    a_recv,
):
    n_head, n_page, n_nodes, n_segs = dims
    h = lax.axis_index("head")
    p = lax.axis_index("page")
    rows = hid.shape[0]
    width = w.shape[1] // 3
    heads = width // HD
    dev_pages, page_len = cache.shape[1], cache.shape[2]
    half = n_page // 2
    sibling = p + 1 - 2 * lax.rem(p, 2)
    slice_rows = wo.shape[0] // SPLIT
    my_slice = lax.rem(p, SPLIT)
    group = p - my_slice

    barrier = pltpu.get_barrier_semaphore()
    for d in range(1, n_head):
        pl.semaphore_signal(
            barrier, inc=1, device_id=(lax.rem(h + d, n_head), p), device_id_type=MESH
        )

    @pl.loop(1, n_page)
    def _(k):
        pl.semaphore_signal(
            barrier, inc=1, device_id=(h, lax.rem(p + k, n_page)), device_id_type=MESH
        )

    wide = hid[...].astype(F32)
    scale = lax.rsqrt(jnp.mean(wide * wide, axis=1, keepdims=True) + EPSILON)
    normed[h] = (wide * scale * gain[...]).astype(BF16)
    pl.semaphore_wait(barrier, n_head - 1 + n_page - 1)

    def x_copy(c, way, target):
        return pltpu.make_async_remote_copy(
            src_ref=normed.at[c],
            dst_ref=normed.at[c],
            send_sem=x_send.at[way, c],
            recv_sem=x_recv.at[c],
            device_id=(target, p),
            device_id_type=MESH,
        )

    def c_copy(src, slot, sem, target):
        return pltpu.make_async_remote_copy(
            src_ref=src,
            dst_ref=cache_all.at[slot],
            send_sem=sem,
            recv_sem=c_recv.at[slot],
            device_id=(h, target),
            device_id_type=MESH,
        )

    def wz_copy(d):
        part = pl.ds(pl.multiple_of(my_slice * slice_rows, slice_rows), slice_rows)
        return pltpu.make_async_remote_copy(
            src_ref=wo.at[part],
            dst_ref=wo_rel.at[d - 1, part],
            send_sem=wz_send.at[d - 1],
            recv_sem=wz_recv.at[d - 1],
            device_id=(lax.rem(h + n_head - d, n_head), p),
            device_id_type=MESH,
        )

    def wp_copy(owner, target):
        part = pl.ds(pl.multiple_of(owner * slice_rows, slice_rows), slice_rows)
        block = wo_rel.at[:, part]
        return pltpu.make_async_remote_copy(
            src_ref=block,
            dst_ref=block,
            send_sem=wp_send.at[target],
            recv_sem=wp_recv.at[owner],
            device_id=(h, group + target),
            device_id_type=MESH,
        )

    def a_copy(c, d):
        return pltpu.make_async_remote_copy(
            src_ref=attn.at[c],
            dst_ref=attn_rel.at[d - 1],
            send_sem=a_send.at[c],
            recv_sem=a_recv.at[d - 1],
            device_id=(c, p),
            device_id_type=MESH,
        )

    @pl.when(h > 0)
    def _():
        x_copy(h, 0, h - 1).start()

    @pl.when(h < n_head - 1)
    def _():
        x_copy(h, 1, h + 1).start()

    @pl.loop(1, half)
    def _(k):
        c_copy(cache, p, c_send.at[k], lax.rem(p + 2 * k, n_page)).start()

    c_copy(cache, p, c_fwd.at[0], sibling).start()
    for d in range(1, n_head):
        wz_copy(d).start()

    lane8 = lax.broadcasted_iota(jnp.int32, (n_segs, 128), 1) & (HD - 1)
    row8 = lax.broadcasted_iota(jnp.int32, (n_segs, 128), 0)
    on_path = lane8 < 0
    for s in range(n_segs):
        low = leaf[0, s]
        mid = parent[low]
        root = parent[mid]
        hit = (lane8 == low) | (lane8 == mid) | (lane8 == root)
        on_path = on_path | (hit & (row8 == s))
    own_lane = lane8 == row8 + (n_nodes + 1)
    used = lane8 < n_nodes + 1 + n_segs
    table_q = jnp.where(used & ~on_path & ~own_lane, 1.0, 0.0)
    table_k = jnp.where(own_lane, -BIG, 0.0)
    tokens = seg.shape[1]
    member = seg[...] == lax.broadcasted_iota(jnp.int32, (n_segs, tokens), 0)
    member = jnp.where(member, 1.0, 0.0)
    turned = (((0,), (0,)), ((), ()))
    ext = lax.dot_general(member, table_q, turned, preferred_element_type=F32)
    qext[...] = ext.reshape(qext.shape)
    ext = lax.dot_general(member, table_k, turned, preferred_element_type=F32)
    kext[...] = ext.reshape(kext.shape)

    def project(c):
        x = normed[c]
        low = lax.broadcasted_iota(jnp.int32, (rows, 128), 1) < HD
        q = dot(x, w[:, :width]).astype(BF16).astype(F32) * HD ** (-0.5)
        k = dot(x, w[:, width : 2 * width])
        v = dot(x, w[:, 2 * width :])
        q_more, k_more = qext[c], kext[c]
        for i in range(heads // 2):
            part = slice(i * 128, (i + 1) * 128)
            qa[2 * i, c] = jnp.where(low, q[:, part], q_more).astype(BF16)
            qa[2 * i + 1, c] = jnp.where(low, q_more, q[:, part]).astype(BF16)
            ka[2 * i, c] = jnp.where(low, k[:, part], k_more).astype(BF16)
            ka[2 * i + 1, c] = jnp.where(low, k_more, k[:, part]).astype(BF16)
            va[2 * i, c] = jnp.where(low, v[:, part], 1.0).astype(BF16)
            va[2 * i + 1, c] = jnp.where(low, 1.0, v[:, part]).astype(BF16)

    def widen_page(g, source, i):
        lane = lax.broadcasted_iota(jnp.int32, (page_len, 128), 1)
        low, slot = lane < HD, lax.broadcasted_iota(jnp.int32, (page_len, 128), 0)
        lane = lane & (HD - 1)
        hidden = (lane == page_node[g]) | ((lane == n_nodes) & (slot >= page_fill[g]))
        more = jnp.where(hidden, -BIG, 0.0)
        for j in range(heads // 2):
            part = slice(j * 128, (j + 1) * 128)
            k = cache_all[source, 0, i, :, part].astype(F32)
            v = cache_all[source, 1, i, :, part].astype(F32)
            kp[2 * j, g] = jnp.where(low, k, more).astype(BF16)
            kp[2 * j + 1, g] = jnp.where(low, more, k).astype(BF16)
            vp[2 * j, g] = jnp.where(low, v, 1.0).astype(BF16)
            vp[2 * j + 1, g] = jnp.where(low, 1.0, v).astype(BF16)

    def take_cache():
        @pl.loop(1, half)
        def _(k):
            source = lax.rem(p + 2 * k, n_page)
            c_copy(cache, source, c_send.at[k], sibling).wait_recv()
            c_copy(cache_all.at[source], source, c_fwd.at[k], sibling).start()

        @pl.loop(0, half)
        def _(k):
            source = lax.rem(sibling + 2 * k, n_page)
            c_copy(cache, source, c_fwd.at[0], sibling).wait_recv()

        cache_all[p] = cache[...]

        @pl.loop(0, n_page)
        def _(source):
            for i in range(dev_pages):
                widen_page(source * dev_pages + i, source, i)

    n_keys = n_page * dev_pages * page_len
    block = min(KEY_BLOCK, n_keys)
    block_pages = block // page_len
    blocks = n_keys // block

    def prefix(c):
        @pl.loop(0, heads)
        def _(i):
            q = qa[i, c]

            def scores(b):
                at = pl.ds(b * block_pages, block_pages)
                s = dot_t(q, kp[i, at].reshape(block, 128))
                return s, vp[i, at].reshape(block, 128)

            s, v = scores(0)
            m = jnp.max(s, axis=1, keepdims=True)
            acc[i, c] = dot(jnp.exp(s - m).astype(BF16), v)
            top[i, c] = jnp.broadcast_to(m, (rows, 128))
            if blocks > 1:

                @pl.loop(1, blocks)
                def _(b):
                    s, v = scores(b)
                    old = top[i, c][:, :1]
                    m = jnp.maximum(old, jnp.max(s, axis=1, keepdims=True))
                    acc[i, c] = acc[i, c] * jnp.exp(old - m) + dot(
                        jnp.exp(s - m).astype(BF16), v
                    )
                    top[i, c] = jnp.broadcast_to(m, (rows, 128))

    def finish(c):
        before = jnp.maximum(c - 1, 0)
        shut = jnp.where(c > 0, 0.0, -BIG)
        low = lax.broadcasted_iota(jnp.int32, (rows, 128), 1) < HD
        at = lax.broadcasted_iota(jnp.int32, (rows, rows), 0)
        seen = lax.broadcasted_iota(jnp.int32, (rows, rows), 1) <= at

        def one(i):
            q = qa[i, c]
            near = jnp.where(seen, dot_t(q, ka[i, c]), -BIG)
            far = dot_t(q, ka[i, before]) + shut
            old = top[i, c][:, :1]
            m = jnp.maximum(old, jnp.max(jnp.maximum(near, far), axis=1, keepdims=True))
            total = (
                acc[i, c] * jnp.exp(old - m)
                + dot(jnp.exp(near - m).astype(BF16), va[i, c])
                + dot(jnp.exp(far - m).astype(BF16), va[i, before])
            )
            return total / pltpu.roll(total, HD, 1)

        for i in range(heads // 2):
            pair = jnp.where(low, one(2 * i), one(2 * i + 1))
            attn[c, :, i * 128 : (i + 1) * 128] = pair.astype(BF16)

        @pl.when(c != h)
        def _():
            a_copy(c, lax.rem(h - c + n_head, n_head)).start()

    def share_w():
        for d in range(1, n_head):
            wz_copy(d).wait_recv()

        @pl.loop(1, SPLIT)
        def _(k):
            wp_copy(my_slice, lax.rem(my_slice + k, SPLIT)).start()

    @pl.loop(0, n_head + 1)
    def _(r):
        left, right = h - r, h + r
        has_left = left >= 0
        has_right = (right < n_head) & (r > 0)

        @pl.when(has_left & (r > 0))
        def _():
            x_copy(left, 1, h).wait_recv()

            @pl.when(h < n_head - 1)
            def _():
                x_copy(left, 1, h + 1).start()

        @pl.when(has_right)
        def _():
            x_copy(right, 0, h).wait_recv()

            @pl.when(h > 0)
            def _():
                x_copy(right, 0, h - 1).start()

        @pl.loop(0, 2)
        def _(j):
            @pl.when((has_left & (j == 0)) | (has_right & (j == 1)))
            def _():
                project(h + (2 * j - 1) * r)

        @pl.when(r == 1)
        def _():
            take_cache()

        @pl.when(r == 2)
        def _():
            share_w()

        @pl.loop(0, 3)
        def _(j):
            ok = has_left & (r > 0) & (j == 0)
            ok = ok | (has_right & (j == 1)) | ((r == 1) & (j == 2))

            @pl.when(ok)
            def _():
                step = jnp.where(j == 2, 0, 2 * j - 1)
                prefix(h + step * r)

        @pl.loop(0, 2)
        def _(j):
            c = jnp.where(j == 0, right, left + 1)
            ok = (has_right & (j == 0)) | ((left + 1 >= 0) & (r > 0) & (j == 1))

            @pl.when(ok)
            def _():
                finish(c)

    total = dot(attn[h], wo[...])

    @pl.loop(1, SPLIT)
    def _(k):
        owner = lax.rem(my_slice + k, SPLIT)
        wp_copy(owner, my_slice).wait_recv()

    for d in range(1, n_head):
        a_copy(h, d).wait_recv()
        total = total + dot(attn_rel[d - 1], wo_rel[d - 1])
    out[...] = total.astype(BF16)

    @pl.loop(0, n_head)
    def _(c):
        @pl.when((h > 0) & (c >= h))
        def _():
            x_copy(c, 0, h).wait_send()

        @pl.when((h < n_head - 1) & (c <= h))
        def _():
            x_copy(c, 1, h).wait_send()

        @pl.when(c != h)
        def _():
            a_copy(c, 1).wait_send()

    @pl.loop(1, half)
    def _(k):
        c_copy(cache, p, c_send.at[k], sibling).wait_send()

    @pl.loop(0, half)
    def _(k):
        c_copy(cache, p, c_fwd.at[k], sibling).wait_send()

    for d in range(1, n_head):
        wz_copy(d).wait_send()

    @pl.loop(1, SPLIT)
    def _(k):
        wp_copy(my_slice, lax.rem(my_slice + k, SPLIT)).wait_send()


def shards(
    n_head,
    n_page,
    hidden_in,
    norm_gain,
    w_qkv,
    w_out,
    cache_kv,
    page_node,
    page_fill,
    node_parent,
    tok_seg,
    req_leaf,
):
    rows, model = hidden_in.shape[1:]
    width = w_qkv.shape[2]
    heads = width // HD
    dev_pages, page_len = cache_kv.shape[1:3]
    pages = n_page * dev_pages
    vmem = pl.BlockSpec(memory_space=pltpu.VMEM)
    smem = pl.BlockSpec(memory_space=pltpu.SMEM)
    dma = pltpu.SemaphoreType.DMA
    dims = (n_head, n_page, node_parent.shape[0], req_leaf.shape[1])
    flops = 2 * n_head * rows * (4 * model * width + 4 * heads * 64 * pages * page_len)
    result = pl.pallas_call(
        functools.partial(kernel, dims),
        out_shape=jax.ShapeDtypeStruct((rows, model), BF16),
        in_specs=[vmem] * 5 + [smem] * 3 + [vmem, smem],
        out_specs=vmem,
        scratch_shapes=[
            pltpu.VMEM((n_head, rows, model), BF16),
            pltpu.VMEM((n_page,) + cache_kv.shape, BF16),
            pltpu.VMEM((n_head - 1, width, model), BF16),
            pltpu.VMEM((heads, n_head, rows, 128), BF16),
            pltpu.VMEM((heads, n_head, rows, 128), BF16),
            pltpu.VMEM((heads, n_head, rows, 128), BF16),
            pltpu.VMEM((heads, pages, page_len, 128), BF16),
            pltpu.VMEM((heads, pages, page_len, 128), BF16),
            pltpu.VMEM((heads, n_head, rows, 128), F32),
            pltpu.VMEM((heads, n_head, rows, 128), F32),
            pltpu.VMEM((n_head, rows, 128), F32),
            pltpu.VMEM((n_head, rows, 128), F32),
            pltpu.VMEM((n_head, rows, width), BF16),
            pltpu.VMEM((n_head - 1, rows, width), BF16),
            dma((2, n_head)),
            dma((n_head,)),
            dma((n_page // 2,)),
            dma((n_page // 2,)),
            dma((n_page,)),
            dma((n_head - 1,)),
            dma((n_head - 1,)),
            dma((SPLIT,)),
            dma((SPLIT,)),
            dma((n_head,)),
            dma((n_head - 1,)),
        ],
        compiler_params=pltpu.CompilerParams(
            collective_id=0, has_side_effects=True, vmem_limit_bytes=60 * 1024 * 1024
        ),
        cost_estimate=pl.CostEstimate(
            flops=flops, bytes_accessed=4 * 1024 * 1024, transcendentals=0
        ),
    )(
        hidden_in[0],
        norm_gain.reshape(1, model),
        w_qkv.reshape(model, 3 * width),
        w_out,
        cache_kv,
        page_node,
        page_fill,
        node_parent,
        tok_seg,
        req_leaf,
    )
    return result[None]


def solution(mesh):
    placed = (
        P("page", "head", None),
        P(),
        P(None, None, "head"),
        P("head", None),
        P(None, "page", None, "head"),
        P(),
        P(),
        P(),
        P("page", None),
        P("page", None),
    )
    body = functools.partial(shards, mesh.shape["head"], mesh.shape["page"])
    return jax.shard_map(
        body, mesh=mesh, in_specs=placed, out_specs=P("page", "head", None), check_vma=False
    )
```

time: 197 us -> 77 us (0.39)
  waiting for transfers between devices: 85.8 us -> 0 us
  Pallas kernels: 0 us -> 71.6 us
  matrix products: 41.7 us -> 0 us
  other arithmetic: 26.1 us -> 0 us
  local copies, waits for them, and re-layouts: 25.2 us -> 5.17 us
  between operations: 13.2 us -> 0.02 us
  loops' own time: 4.01 us -> 0 us
    pallas_call x0 -> x1, Pallas kernels: none -> 71.6 us  [shards(): pl.pallas_call(functools.partial(kernel, dims), out_shape=jax.ShapeDtypeS...]
    reduce_scatter x1 -> x0, waiting for transfers between devices: 42.8 us -> none  [shards(): lax.psum_scatter(jnp.dot(attention, w_out, preferred_element_type=jnp.flo...]
    all_gather x2 -> x0, waiting for transfers between devices: 42.3 us -> none  [the longest x1 42.3 us: shards(): lax.all_gather(normed, 'head', axis=0, tiled=True)]
    dot_general x14 -> x0, matrix products: 41.7 us -> none  [the longest x4 14.6 us: one_step(): jnp.einsum('hqk,khd->hqd', weights.astype(jnp.bfloat16), value_block, pre...]
    reduce_sum x10 -> x0, other arithmetic: 17.8 us -> none  [the longest x4 8.44 us: one_step(): row_sum = row_sum * rescale + jnp.sum(weights, axis=2)]
    while x22 -> x0, local copies, waits for them, and re-layouts: 8.56 us -> none  [the longest x2 4.68 us: shards(): lax.scan(one_step, initial, (key_blocks, value_blocks, key_nodes, key_val...]
    another operation x2 -> x0, local copies, waits for them, and re-layouts: 6.63 us -> none  [the longest x1 3.32 us: shards(): shard_piece[1].reshape(step_count, block_keys, group_heads, head_size)]
    slice x2 -> x0, local copies, waits for them, and re-layouts: 4.04 us -> none  [the longest x1 3.13 us: shards(): shard_piece[1].reshape(step_count, block_keys, group_heads, head_size)]
  transfers between devices with their start and end apart: 3 -> 0, of which waited for: 2 -> 0; matrix products, arithmetic and copies ran while one was open for 16% -> 0% of each run, Pallas kernels for 0% -> 0%
where the time goes in v1:
time: 77 us; the launch traced here: 76.8 us
  Pallas kernels  71.6 us (93%)
  local copies, waits for them, and re-layouts  5.17 us (7%)
    pallas_call x1, Pallas kernels, shards(): pl.pallas_call(functools.partial(kernel, dims), out_shape=jax.ShapeDtypeS...  71.6 us
    unnamed x2, local copies, waits for them, and re-layouts  3.58 us
    reshape x1, local copies, waits for them, and re-layouts, shards(): w_qkv.reshape(model, 3 * width)  1.6 us

profile of v1, /device:TPU:0, one launch (start us, length us, event | category | flops | bytes accessed | tf_op | source)
XLA Modules:
  0.0 76.8 jit_solution(16295360902370057176)
XLA Ops:
  0.0 1.7 %copy.12 = bf16[1024,3,256]{0,2,1:T(8,128)(2,1)S(1)} copy(bf16[1024,3,256]{2,0,1:T(8,128)(2,1)} %param.12) | data formatting | bytes 3145728 | tf_op args[2]
  1.7 1.6 %copy.13.w = bf16[1024,768]{1,0:T(8,128)(2,1)} copy(bf16[1024,768]{0,1:T(8,128)(2,1)S(1)} %bitcast.4) | data formatting | bytes 3145728 | tf_op jit(solution)/shard_map/reshape | solution.py:467
  3.3 71.6 %shard_map.100 = bf16[256,1024]{1,0:T(8,128)(2,1)} custom-call(bf16[256,1024]{1,0:T(8,128)(2,1)} %bitcast.6, f32[1,1024]{1,0:T(1,128)} %bitcast.7, bf16[1024,768]{1,0:T(8,128)(2,1)} %copy.13.w, bf16[256,1024]{1,0:T(8,128)(2,1)} %wo.1, bf16[2,2,128,256]{3,2,1,0:T(8,128)(2,1)} %cache.1, s32[16]{0:T(128)} %page_node.1, s32[16]{0:T(128)} %page_fill.1, s32[7]{0:T(128)} %parent.1, ...), custom_call_target="tpu_custom_call" | custom-call | flops 6442450944 | bytes 4194304 | tf_op jit(solution)/shard_map/pallas_call | solution.py:426
  74.9 1.9 %copy.15 = bf16[1,256,1024]{2,1,0:T(8,128)(2,1)} copy(bf16[1,256,1024]{2,1,0:T(8,128)(2,1)} %bitcast.5) | data formatting | bytes 1048576

commit v2 on v1

--- a/solution.py
+++ b/solution.py
@@ -25,11 +25,15 @@
     return jnp.dot(a, b, preferred_element_type=F32)
 
 
+def weigh(s, m):
+    return jnp.exp((s - m).astype(BF16))
+
+
 def kernel(
     dims,
     hid,
     gain,
-    w,
+    w_hbm,
     wo,
     cache,
     page_node,
@@ -52,6 +56,8 @@
     kext,
     attn,
     attn_rel,
+    w,
+    w_sem,
     x_send,
     x_recv,
     c_send,
@@ -68,7 +74,7 @@
     h = lax.axis_index("head")
     p = lax.axis_index("page")
     rows = hid.shape[0]
-    width = w.shape[1] // 3
+    width = w_hbm.shape[2]
     heads = width // HD
     dev_pages, page_len = cache.shape[1], cache.shape[2]
     half = n_page // 2
@@ -76,6 +82,9 @@
     slice_rows = wo.shape[0] // SPLIT
     my_slice = lax.rem(p, SPLIT)
     group = p - my_slice
+
+    w_copy = pltpu.make_async_copy(w_hbm, w, w_sem)
+    w_copy.start()
 
     barrier = pltpu.get_barrier_semaphore()
     for d in range(1, n_head):
@@ -188,9 +197,9 @@
     def project(c):
         x = normed[c]
         low = lax.broadcasted_iota(jnp.int32, (rows, 128), 1) < HD
-        q = dot(x, w[:, :width]).astype(BF16).astype(F32) * HD ** (-0.5)
-        k = dot(x, w[:, width : 2 * width])
-        v = dot(x, w[:, 2 * width :])
+        q = dot(x, w[0]).astype(BF16).astype(F32) * HD ** (-0.5)
+        k = dot(x, w[1])
+        v = dot(x, w[2])
         q_more, k_more = qext[c], kext[c]
         for i in range(heads // 2):
             part = slice(i * 128, (i + 1) * 128)
@@ -240,31 +249,33 @@
     block_pages = block // page_len
     blocks = n_keys // block
 
+    def prefix_head(c, i):
+        q = qa[i, c]
+
+        def scores(b):
+            at = pl.ds(b * block_pages, block_pages)
+            s = dot_t(q, kp[i, at].reshape(block, 128))
+            return s, vp[i, at].reshape(block, 128)
+
+        s, v = scores(0)
+        m = jnp.max(s, axis=1, keepdims=True)
+        acc[i, c] = dot(weigh(s, m), v)
+        top[i, c] = jnp.broadcast_to(m, (rows, 128))
+        if blocks > 1:
+
+            @pl.loop(1, blocks)
+            def _(b):
+                s, v = scores(b)
+                old = top[i, c][:, :1]
+                m = jnp.maximum(old, jnp.max(s, axis=1, keepdims=True))
+                acc[i, c] = acc[i, c] * jnp.exp(old - m) + dot(weigh(s, m), v)
+                top[i, c] = jnp.broadcast_to(m, (rows, 128))
+
     def prefix(c):
-        @pl.loop(0, heads)
-        def _(i):
-            q = qa[i, c]
-
-            def scores(b):
-                at = pl.ds(b * block_pages, block_pages)
-                s = dot_t(q, kp[i, at].reshape(block, 128))
-                return s, vp[i, at].reshape(block, 128)
-
-            s, v = scores(0)
-            m = jnp.max(s, axis=1, keepdims=True)
-            acc[i, c] = dot(jnp.exp(s - m).astype(BF16), v)
-            top[i, c] = jnp.broadcast_to(m, (rows, 128))
-            if blocks > 1:
-
-                @pl.loop(1, blocks)
-                def _(b):
-                    s, v = scores(b)
-                    old = top[i, c][:, :1]
-                    m = jnp.maximum(old, jnp.max(s, axis=1, keepdims=True))
-                    acc[i, c] = acc[i, c] * jnp.exp(old - m) + dot(
-                        jnp.exp(s - m).astype(BF16), v
-                    )
-                    top[i, c] = jnp.broadcast_to(m, (rows, 128))
+        @pl.loop(0, heads // 2)
+        def _(pair):
+            for i in (2 * pair, 2 * pair + 1):
+                prefix_head(c, i)
 
     def finish(c):
         before = jnp.maximum(c - 1, 0)
@@ -281,8 +292,8 @@
             m = jnp.maximum(old, jnp.max(jnp.maximum(near, far), axis=1, keepdims=True))
             total = (
                 acc[i, c] * jnp.exp(old - m)
-                + dot(jnp.exp(near - m).astype(BF16), va[i, c])
-                + dot(jnp.exp(far - m).astype(BF16), va[i, before])
+                + dot(weigh(near, m), va[i, c])
+                + dot(weigh(far, m), va[i, before])
             )
             return total / pltpu.roll(total, HD, 1)
 
@@ -302,7 +313,9 @@
         def _(k):
             wp_copy(my_slice, lax.rem(my_slice + k, SPLIT)).start()
 
-    @pl.loop(0, n_head + 1)
+    w_copy.wait()
+
+    @pl.loop(0, n_head)
     def _(r):
         left, right = h - r, h + r
         has_left = left >= 0
@@ -338,22 +351,22 @@
         def _():
             share_w()
 
-        @pl.loop(0, 3)
+        @pl.loop(0, 4)
         def _(j):
-            ok = has_left & (r > 0) & (j == 0)
-            ok = ok | (has_right & (j == 1)) | ((r == 1) & (j == 2))
+            side = 2 * (j & 1) - 1
+            far = jnp.where(r == 1, 0, jnp.where(j < 2, r - 1, r))
+            c = h + side * far
+            ok = ((r == 1) & (j == 0)) | ((r == 2) & (c >= 0) & (c < n_head))
+            ok = ok | ((r > 2) & (j >= 2) & (c >= 0) & (c < n_head))
 
             @pl.when(ok)
             def _():
-                step = jnp.where(j == 2, 0, 2 * j - 1)
-                prefix(h + step * r)
-
-        @pl.loop(0, 2)
-        def _(j):
-            c = jnp.where(j == 0, right, left + 1)
-            ok = (has_right & (j == 0)) | ((left + 1 >= 0) & (r > 0) & (j == 1))
-
-            @pl.when(ok)
+                prefix(c)
+
+            ripe = ok & ((j != 2) | (c == 0))
+            ripe = ripe | ((r > 2) & (j == 0) & (c > 0))
+
+            @pl.when(ripe)
             def _():
                 finish(c)
 
@@ -426,7 +439,7 @@
     result = pl.pallas_call(
         functools.partial(kernel, dims),
         out_shape=jax.ShapeDtypeStruct((rows, model), BF16),
-        in_specs=[vmem] * 5 + [smem] * 3 + [vmem, smem],
+        in_specs=[vmem] * 2 + [pl.BlockSpec(memory_space=pl.ANY)] + [vmem] * 2 + [smem] * 3 + [vmem, smem],
         out_specs=vmem,
         scratch_shapes=[
             pltpu.VMEM((n_head, rows, model), BF16),
@@ -443,6 +456,8 @@
             pltpu.VMEM((n_head, rows, 128), F32),
             pltpu.VMEM((n_head, rows, width), BF16),
             pltpu.VMEM((n_head - 1, rows, width), BF16),
+            pltpu.VMEM((3, model, width), BF16),
+            dma,
             dma((2, n_head)),
             dma((n_head,)),
             dma((n_page // 2,)),
@@ -464,7 +479,7 @@
     )(
         hidden_in[0],
         norm_gain.reshape(1, model),
-        w_qkv.reshape(model, 3 * width),
+        jnp.transpose(w_qkv, (1, 0, 2)),
         w_out,
         cache_kv,
         page_node,

time: 77 us -> 65 us (0.84)
  Pallas kernels: 71.6 us -> 63 us
  local copies, waits for them, and re-layouts: 5.17 us -> 1.87 us
    pallas_call x1, Pallas kernels: 71.6 us -> 63 us  [shards(): pl.pallas_call(functools.partial(kernel, dims), out_shape=jax.ShapeDtypeS...]
    unnamed x2 -> x1, local copies, waits for them, and re-layouts: 3.58 us -> 1.87 us
    reshape x1 -> x0, local copies, waits for them, and re-layouts: 1.6 us -> none  [shards(): w_qkv.reshape(model, 3 * width)]
where the time goes in v2:
time: 65 us; the launch traced here: 64.9 us
  Pallas kernels  63 us (97%)
  local copies, waits for them, and re-layouts  1.87 us (3%)
    pallas_call x1, Pallas kernels, shards(): pl.pallas_call(functools.partial(kernel, dims), out_shape=jax.ShapeDtypeS...  63 us
    unnamed x1, local copies, waits for them, and re-layouts  1.87 us

profile of v2, /device:TPU:0, one launch (start us, length us, event | category | flops | bytes accessed | tf_op | source)
XLA Modules:
  0.0 64.9 jit_solution(11294162593117503716)
XLA Ops:
  0.0 63.0 %shard_map.100 = bf16[256,1024]{1,0:T(8,128)(2,1)} custom-call(bf16[256,1024]{1,0:T(8,128)(2,1)} %bitcast.6, f32[1,1024]{1,0:T(1,128)} %bitcast.7, bf16[3,1024,256]{2,1,0:T(8,128)(2,1)} %bitcast.5, bf16[256,1024]{1,0:T(8,128)(2,1)} %wo.1, bf16[2,2,128,256]{3,2,1,0:T(8,128)(2,1)} %cache.1, s32[16]{0:T(128)} %page_node.1, s32[16]{0:T(128)} %page_fill.1, ...), custom_call_target="tpu_custom_call" | custom-call | flops 6442450944 | bytes 4194304 | tf_op jit(solution)/shard_map/pallas_call | solution.py:439
  63.0 1.9 %copy.12 = bf16[1,256,1024]{2,1,0:T(8,128)(2,1)} copy(bf16[1,256,1024]{2,1,0:T(8,128)(2,1)} %bitcast.4) | data formatting | bytes 1048576

commit v3 on v2

--- a/solution.py
+++ b/solution.py
@@ -78,6 +78,16 @@
     heads = width // HD
     dev_pages, page_len = cache.shape[1], cache.shape[2]
     half = n_page // 2
+    pair, core = p // 2, lax.rem(p, 2)
+
+    def chip(k):
+        outer = lax.rem(pair // 2 + k // 2, half // 2)
+        return 2 * outer + lax.rem(pair + k, 2)
+
+    def chip_back(k):
+        outer = lax.rem(pair // 2 + half // 2 - k // 2, half // 2)
+        return 2 * outer + lax.rem(pair + k, 2)
+
     sibling = p + 1 - 2 * lax.rem(p, 2)
     slice_rows = wo.shape[0] // SPLIT
     my_slice = lax.rem(p, SPLIT)
@@ -166,7 +176,7 @@
 
     @pl.loop(1, half)
     def _(k):
-        c_copy(cache, p, c_send.at[k], lax.rem(p + 2 * k, n_page)).start()
+        c_copy(cache, p, c_send.at[k], 2 * chip_back(k) + core).start()
 
     c_copy(cache, p, c_fwd.at[0], sibling).start()
     for d in range(1, n_head):
@@ -226,50 +236,52 @@
             vp[2 * j + 1, g] = jnp.where(low, 1.0, v).astype(BF16)
 
     def take_cache():
-        @pl.loop(1, half)
-        def _(k):
-            source = lax.rem(p + 2 * k, n_page)
-            c_copy(cache, source, c_send.at[k], sibling).wait_recv()
-            c_copy(cache_all.at[source], source, c_fwd.at[k], sibling).start()
+        cache_all[p] = cache[...]
+        for i in range(heads):
+            acc[i, h] = jnp.zeros((rows, 128), F32)
+            top[i, h] = jnp.full((rows, 128), -3 * BIG, F32)
 
         @pl.loop(0, half)
         def _(k):
-            source = lax.rem(sibling + 2 * k, n_page)
-            c_copy(cache, source, c_fwd.at[0], sibling).wait_recv()
-
-        cache_all[p] = cache[...]
-
-        @pl.loop(0, n_page)
-        def _(source):
-            for i in range(dev_pages):
-                widen_page(source * dev_pages + i, source, i)
+            first = 2 * chip(k)
+            source, other = first + core, first + 1 - core
+
+            @pl.when(k > 0)
+            def _():
+                c_copy(cache, source, c_send.at[k], sibling).wait_recv()
+                c_copy(cache_all.at[source], source, c_fwd.at[k], sibling).start()
+
+            c_copy(cache, other, c_fwd.at[0], sibling).wait_recv()
+            for n in range(2):
+                for i in range(dev_pages):
+                    widen_page((first + n) * dev_pages + i, first + n, i)
+            for i in range(heads):
+                at = pl.ds(first * dev_pages, 2 * dev_pages)
+                extend(h, i, at, 2 * dev_pages * page_len)
 
     n_keys = n_page * dev_pages * page_len
     block = min(KEY_BLOCK, n_keys)
     block_pages = block // page_len
     blocks = n_keys // block
 
+    def extend(c, i, at, size):
+        s = dot_t(qa[i, c], kp[i, at].reshape(size, 128))
+        old = top[i, c][:, :1]
+        m = jnp.maximum(old, jnp.max(s, axis=1, keepdims=True))
+        more = dot(weigh(s, m), vp[i, at].reshape(size, 128))
+        acc[i, c] = acc[i, c] * jnp.exp(old - m) + more
+        top[i, c] = jnp.broadcast_to(m, (rows, 128))
+
     def prefix_head(c, i):
-        q = qa[i, c]
-
-        def scores(b):
-            at = pl.ds(b * block_pages, block_pages)
-            s = dot_t(q, kp[i, at].reshape(block, 128))
-            return s, vp[i, at].reshape(block, 128)
-
-        s, v = scores(0)
+        s = dot_t(qa[i, c], kp[i, :block_pages].reshape(block, 128))
         m = jnp.max(s, axis=1, keepdims=True)
-        acc[i, c] = dot(weigh(s, m), v)
+        acc[i, c] = dot(weigh(s, m), vp[i, :block_pages].reshape(block, 128))
         top[i, c] = jnp.broadcast_to(m, (rows, 128))
         if blocks > 1:
 
             @pl.loop(1, blocks)
             def _(b):
-                s, v = scores(b)
-                old = top[i, c][:, :1]
-                m = jnp.maximum(old, jnp.max(s, axis=1, keepdims=True))
-                acc[i, c] = acc[i, c] * jnp.exp(old - m) + dot(weigh(s, m), v)
-                top[i, c] = jnp.broadcast_to(m, (rows, 128))
+                extend(c, i, pl.ds(b * block_pages, block_pages), block)
 
     def prefix(c):
         @pl.loop(0, heads // 2)
@@ -343,7 +355,7 @@
             def _():
                 project(h + (2 * j - 1) * r)
 
-        @pl.when(r == 1)
+        @pl.when(r == 0)
         def _():
             take_cache()
 
@@ -353,20 +365,20 @@
 
         @pl.loop(0, 4)
         def _(j):
-            side = 2 * (j & 1) - 1
-            far = jnp.where(r == 1, 0, jnp.where(j < 2, r - 1, r))
-            c = h + side * far
-            ok = ((r == 1) & (j == 0)) | ((r == 2) & (c >= 0) & (c < n_head))
-            ok = ok | ((r > 2) & (j >= 2) & (c >= 0) & (c < n_head))
-
-            @pl.when(ok)
+            c = jnp.where(j == 0, h, jnp.where(j == 1, h + r, jnp.where(j == 2, h - r + 1, h - r)))
+            inside = (c >= 0) & (c < n_head) & (r > 0)
+            last = h == n_head - 1
+            begin = (j == 1) | ((j == 2) & (r == 2) & (h < n_head - 1))
+            begin = begin | ((j == 3) & ((r > 1) | last))
+            end = ((j == 0) & (r == 1)) | (j == 1)
+            end = end | ((j == 2) & ((r == 2) | ((r > 2) & (c > 0))))
+            end = end | ((j == 3) & (r > 1) & (c == 0))
+
+            @pl.when(inside & begin)
             def _():
                 prefix(c)
 
-            ripe = ok & ((j != 2) | (c == 0))
-            ripe = ripe | ((r > 2) & (j == 0) & (c > 0))
-
-            @pl.when(ripe)
+            @pl.when(inside & end)
             def _():
                 finish(c)
 

time: 65 us -> 70.6 us (1.086)
  Pallas kernels: 63 us -> 68.6 us
    pallas_call x1, Pallas kernels: 63 us -> 68.6 us  [shards(): pl.pallas_call(functools.partial(kernel, dims), out_shape=jax.ShapeDtypeS...]
where the time goes in v3:
time: 70.6 us; the launch traced here: 70.4 us
  Pallas kernels  68.6 us (97%)
  local copies, waits for them, and re-layouts  1.87 us (3%)
    pallas_call x1, Pallas kernels, shards(): pl.pallas_call(functools.partial(kernel, dims), out_shape=jax.ShapeDtypeS...  68.6 us
    unnamed x1, local copies, waits for them, and re-layouts  1.87 us

profile of v3, /device:TPU:0, one launch (start us, length us, event | category | flops | bytes accessed | tf_op | source)
XLA Modules:
  0.0 70.4 jit_solution(10145741336191319808)
XLA Ops:
  0.0 68.6 %shard_map.100 = bf16[256,1024]{1,0:T(8,128)(2,1)} custom-call(bf16[256,1024]{1,0:T(8,128)(2,1)} %bitcast.6, f32[1,1024]{1,0:T(1,128)} %bitcast.7, bf16[3,1024,256]{2,1,0:T(8,128)(2,1)} %bitcast.5, bf16[256,1024]{1,0:T(8,128)(2,1)} %wo.1, bf16[2,2,128,256]{3,2,1,0:T(8,128)(2,1)} %cache.1, s32[16]{0:T(128)} %page_node.1, s32[16]{0:T(128)} %page_fill.1, ...), custom_call_target="tpu_custom_call" | custom-call | flops 6442450944 | bytes 4194304 | tf_op jit(solution)/shard_map/pallas_call | solution.py:451
  68.6 1.9 %copy.12 = bf16[1,256,1024]{2,1,0:T(8,128)(2,1)} copy(bf16[1,256,1024]{2,1,0:T(8,128)(2,1)} %bitcast.4) | data formatting | bytes 1048576

commit v4 on v3

--- a/solution.py
+++ b/solution.py
@@ -226,20 +226,18 @@
         lane = lane & (HD - 1)
         hidden = (lane == page_node[g]) | ((lane == n_nodes) & (slot >= page_fill[g]))
         more = jnp.where(hidden, -BIG, 0.0)
+        at = pl.ds(pl.multiple_of(g * page_len, page_len), page_len)
         for j in range(heads // 2):
             part = slice(j * 128, (j + 1) * 128)
             k = cache_all[source, 0, i, :, part].astype(F32)
             v = cache_all[source, 1, i, :, part].astype(F32)
-            kp[2 * j, g] = jnp.where(low, k, more).astype(BF16)
-            kp[2 * j + 1, g] = jnp.where(low, more, k).astype(BF16)
+            kp[2 * j, :, at] = jnp.where(low, k, more).T.astype(BF16)
+            kp[2 * j + 1, :, at] = jnp.where(low, more, k).T.astype(BF16)
             vp[2 * j, g] = jnp.where(low, v, 1.0).astype(BF16)
             vp[2 * j + 1, g] = jnp.where(low, 1.0, v).astype(BF16)
 
     def take_cache():
         cache_all[p] = cache[...]
-        for i in range(heads):
-            acc[i, h] = jnp.zeros((rows, 128), F32)
-            top[i, h] = jnp.full((rows, 128), -3 * BIG, F32)
 
         @pl.loop(0, half)
         def _(k):
@@ -255,25 +253,14 @@
             for n in range(2):
                 for i in range(dev_pages):
                     widen_page((first + n) * dev_pages + i, first + n, i)
-            for i in range(heads):
-                at = pl.ds(first * dev_pages, 2 * dev_pages)
-                extend(h, i, at, 2 * dev_pages * page_len)
 
     n_keys = n_page * dev_pages * page_len
     block = min(KEY_BLOCK, n_keys)
     block_pages = block // page_len
     blocks = n_keys // block
 
-    def extend(c, i, at, size):
-        s = dot_t(qa[i, c], kp[i, at].reshape(size, 128))
-        old = top[i, c][:, :1]
-        m = jnp.maximum(old, jnp.max(s, axis=1, keepdims=True))
-        more = dot(weigh(s, m), vp[i, at].reshape(size, 128))
-        acc[i, c] = acc[i, c] * jnp.exp(old - m) + more
-        top[i, c] = jnp.broadcast_to(m, (rows, 128))
-
     def prefix_head(c, i):
-        s = dot_t(qa[i, c], kp[i, :block_pages].reshape(block, 128))
+        s = dot(qa[i, c], kp[i, :, :block])
         m = jnp.max(s, axis=1, keepdims=True)
         acc[i, c] = dot(weigh(s, m), vp[i, :block_pages].reshape(block, 128))
         top[i, c] = jnp.broadcast_to(m, (rows, 128))
@@ -281,7 +268,12 @@
 
             @pl.loop(1, blocks)
             def _(b):
-                extend(c, i, pl.ds(b * block_pages, block_pages), block)
+                s = dot(qa[i, c], kp[i, :, pl.ds(pl.multiple_of(b * block, block), block)])
+                old = top[i, c][:, :1]
+                m = jnp.maximum(old, jnp.max(s, axis=1, keepdims=True))
+                v = vp[i, pl.ds(b * block_pages, block_pages)].reshape(block, 128)
+                acc[i, c] = acc[i, c] * jnp.exp(old - m) + dot(weigh(s, m), v)
+                top[i, c] = jnp.broadcast_to(m, (rows, 128))
 
     def prefix(c):
         @pl.loop(0, heads // 2)
@@ -365,20 +357,20 @@
 
         @pl.loop(0, 4)
         def _(j):
-            c = jnp.where(j == 0, h, jnp.where(j == 1, h + r, jnp.where(j == 2, h - r + 1, h - r)))
-            inside = (c >= 0) & (c < n_head) & (r > 0)
-            last = h == n_head - 1
-            begin = (j == 1) | ((j == 2) & (r == 2) & (h < n_head - 1))
-            begin = begin | ((j == 3) & ((r > 1) | last))
-            end = ((j == 0) & (r == 1)) | (j == 1)
-            end = end | ((j == 2) & ((r == 2) | ((r > 2) & (c > 0))))
-            end = end | ((j == 3) & (r > 1) & (c == 0))
-
-            @pl.when(inside & begin)
+            side = 2 * (j & 1) - 1
+            far = jnp.where(r == 1, 0, jnp.where(j < 2, r - 1, r))
+            c = h + side * far
+            ok = ((r == 1) & (j == 0)) | ((r == 2) & (c >= 0) & (c < n_head))
+            ok = ok | ((r > 2) & (j >= 2) & (c >= 0) & (c < n_head))
+
+            @pl.when(ok)
             def _():
                 prefix(c)
 
-            @pl.when(inside & end)
+            ripe = ok & ((j != 2) | (c == 0))
+            ripe = ripe | ((r > 2) & (j == 0) & (c > 0))
+
+            @pl.when(ripe)
             def _():
                 finish(c)
 
@@ -460,7 +452,7 @@
             pltpu.VMEM((heads, n_head, rows, 128), BF16),
             pltpu.VMEM((heads, n_head, rows, 128), BF16),
             pltpu.VMEM((heads, n_head, rows, 128), BF16),
-            pltpu.VMEM((heads, pages, page_len, 128), BF16),
+            pltpu.VMEM((heads, 128, pages * page_len), BF16),
             pltpu.VMEM((heads, pages, page_len, 128), BF16),
             pltpu.VMEM((heads, n_head, rows, 128), F32),
             pltpu.VMEM((heads, n_head, rows, 128), F32),

time: 70.6 us -> 65.1 us (0.922)
  Pallas kernels: 68.6 us -> 63 us
    pallas_call x1, Pallas kernels: 68.6 us -> 63 us  [shards(): pl.pallas_call(functools.partial(kernel, dims), out_shape=jax.ShapeDtypeS...]
where the time goes in v4:
time: 65.1 us; the launch traced here: 64.9 us
  Pallas kernels  63 us (97%)
  local copies, waits for them, and re-layouts  1.87 us (3%)
    pallas_call x1, Pallas kernels, shards(): pl.pallas_call(functools.partial(kernel, dims), out_shape=jax.ShapeDtypeS...  63 us
    unnamed x1, local copies, waits for them, and re-layouts  1.87 us

profile of v4, /device:TPU:0, one launch (start us, length us, event | category | flops | bytes accessed | tf_op | source)
XLA Modules:
  0.0 64.9 jit_solution(13842521265835187636)
XLA Ops:
  0.0 63.0 %shard_map.100 = bf16[256,1024]{1,0:T(8,128)(2,1)} custom-call(bf16[256,1024]{1,0:T(8,128)(2,1)} %bitcast.6, f32[1,1024]{1,0:T(1,128)} %bitcast.7, bf16[3,1024,256]{2,1,0:T(8,128)(2,1)} %bitcast.5, bf16[256,1024]{1,0:T(8,128)(2,1)} %wo.1, bf16[2,2,128,256]{3,2,1,0:T(8,128)(2,1)} %cache.1, s32[16]{0:T(128)} %page_node.1, s32[16]{0:T(128)} %page_fill.1, ...), custom_call_target="tpu_custom_call" | custom-call | flops 6442450944 | bytes 4194304 | tf_op jit(solution)/shard_map/pallas_call | solution.py:443
  63.0 1.9 %copy.12 = bf16[1,256,1024]{2,1,0:T(8,128)(2,1)} copy(bf16[1,256,1024]{2,1,0:T(8,128)(2,1)} %bitcast.4) | data formatting | bytes 1048576

commit v5 on v4

--- a/solution.py
+++ b/solution.py
@@ -351,7 +351,7 @@
         def _():
             take_cache()
 
-        @pl.when(r == 2)
+        @pl.when(r == 1)
         def _():
             share_w()
 

time: 65.1 us -> 65.1 us (level)
  no operation moved by 1% of the time
where the time goes in v5:
time: 65.1 us; the launch traced here: 65 us
  Pallas kernels  63.1 us (97%)
  local copies, waits for them, and re-layouts  1.87 us (3%)
    pallas_call x1, Pallas kernels, shards(): pl.pallas_call(functools.partial(kernel, dims), out_shape=jax.ShapeDtypeS...  63.1 us
    unnamed x1, local copies, waits for them, and re-layouts  1.87 us

profile of v5, /device:TPU:0, one launch (start us, length us, event | category | flops | bytes accessed | tf_op | source)
XLA Modules:
  0.0 65.0 jit_solution(8299177600516571375)
XLA Ops:
  0.0 63.1 %shard_map.100 = bf16[256,1024]{1,0:T(8,128)(2,1)} custom-call(bf16[256,1024]{1,0:T(8,128)(2,1)} %bitcast.6, f32[1,1024]{1,0:T(1,128)} %bitcast.7, bf16[3,1024,256]{2,1,0:T(8,128)(2,1)} %bitcast.5, bf16[256,1024]{1,0:T(8,128)(2,1)} %wo.1, bf16[2,2,128,256]{3,2,1,0:T(8,128)(2,1)} %cache.1, s32[16]{0:T(128)} %page_node.1, s32[16]{0:T(128)} %page_fill.1, ...), custom_call_target="tpu_custom_call" | custom-call | flops 6442450944 | bytes 4194304 | tf_op jit(solution)/shard_map/pallas_call | solution.py:443
  63.1 1.9 %copy.12 = bf16[1,256,1024]{2,1,0:T(8,128)(2,1)} copy(bf16[1,256,1024]{2,1,0:T(8,128)(2,1)} %bitcast.4) | data formatting | bytes 1048576
